TPU v7x, 32 devices: a whole 2x2x4 slice. The times are simulated.
32 devices in a mesh: row: 8 (over z, y), col: 4 (over x, core).
Axes of the slice: x: 2, y: 2, z: 4, core: 2. Of those that a mesh axis runs over, the one named last changes fastest.
Arguments:
- tile_values: bfloat16 [64, 192, 128, 128], P('row', 'col'), may hold values from -0.078125 to 0.078125
- block_cols: int32 [64, 192], P('row', 'col'), may hold values from 0 to 4096, as said below
- primal_start: float32 [524288], P('col'), may hold values from -6 to 6
- dual_start: float32 [8192], P('row'), may hold values from -6 to 6
- cost_vector: float32 [524288], P('col'), may hold values from -6 to 6
- lower_bound: float32 [524288], P('col'), may hold values from -1 to -0.1
- upper_bound: float32 [524288], P('col'), may hold values from 0.1 to 1
- var_kinds: int32 [524288], P('col'), may hold values from 0 to 2
- right_side: float32 [8192], P('row'), may hold values from -6 to 6
- row_kinds: int32 [8192], P('row'), may hold values from 0 to 1
Outputs:
- primal_final: float32 [524288], P('col')
- dual_final: float32 [8192], P('row')
Inputs may be any that keep to these rules, and one draw needn't show every extreme that they name: `block_cols`: slots holding 4096 are empty; in each row band the live slots of index c of col come first and name column blocks c * 1024 to c * 1024 + 1023; one index of col holds all 48 slots live for some band.
All inputs are finite; a program needn't handle non-finite values.
Results may differ from a plain program's by a relative error of at most 0.002.
Values may be sent and summed in bfloat16 or wider, within the bound.
A program may use at most 64 MiB of HBM per device.

v0:
```python
import jax
import jax.numpy as jnp
from jax import lax
from jax.sharding import PartitionSpec as P

step_size = 0.8
epsilon = 1e-06


def project_primal(vector, lower_bound, upper_bound, var_kinds):
    raised = jnp.where(var_kinds >= 1, jnp.maximum(vector, lower_bound), vector)
    return jnp.where(var_kinds == 2, jnp.minimum(raised, upper_bound), raised)


def project_dual(vector, row_kinds):
    return jnp.where(row_kinds == 1, jnp.maximum(vector, 0.0), vector)


def per_device(
    tile_values,
    block_cols,
    primal_start,
    dual_start,
    cost_vector,
    lower_bound,
    upper_bound,
    var_kinds,
    right_side,
    row_kinds,
):
    band_count, slot_count, tile_width, _ = tile_values.shape
    col_devices = lax.axis_size("col")
    local_len = primal_start.shape[0]
    blocks_dev = local_len // tile_width
    total_blocks = blocks_dev * col_devices
    row_place = lax.axis_index("row")
    col_place = lax.axis_index("col")
    segment_ids = jnp.where(
        block_cols == total_blocks, blocks_dev, block_cols - col_place * blocks_dev
    )
    flat_ids = segment_ids.reshape(-1)

    def transpose_partial(dual_half):
        contrib = jnp.einsum(
            "bsij,bi->bsj",
            tile_values,
            dual_half.reshape(band_count, tile_width),
            preferred_element_type=jnp.float32,
        )
        summed = jax.ops.segment_sum(
            contrib.reshape(band_count * slot_count, tile_width),
            flat_ids,
            num_segments=blocks_dev + 1,
        )
        return summed[:blocks_dev].reshape(-1)

    def forward_total(shard_bar):
        padded = jnp.concatenate(
            [shard_bar.reshape(blocks_dev, tile_width), jnp.zeros((1, tile_width), jnp.bfloat16)],
            axis=0,
        )
        picked = padded[segment_ids]
        partial_value = jnp.einsum(
            "bsij,bsj->bi", tile_values, picked, preferred_element_type=jnp.float32
        ).reshape(-1)
        return lax.psum(partial_value, "col")

    def iterate(primal, dual, primal_weight):
        primal_step = step_size / primal_weight
        dual_step = step_size * primal_weight
        partial_value = transpose_partial(dual.astype(jnp.bfloat16))
        col_product = lax.psum(partial_value, "row")
        primal_next = project_primal(
            primal - primal_step * (cost_vector - col_product), lower_bound, upper_bound, var_kinds
        )
        extrapolated = (2.0 * primal_next - primal).astype(jnp.bfloat16)
        row_product = forward_total(extrapolated)
        dual_next = project_dual(dual + dual_step * (right_side - row_product), row_kinds)
        return (primal_next, dual_next)

    primal_one, dual_one = iterate(primal_start, dual_start, 1.0)
    primal_term = jnp.sum((primal_one - primal_start) ** 2)
    dual_term = jnp.sum((dual_one - dual_start) ** 2)
    primal_share = jnp.where(row_place == 0, primal_term, 0.0)
    dual_share = jnp.where(col_place == 0, dual_term, 0.0)
    primal_moved, dual_moved = lax.psum((primal_share, dual_share), ("row", "col"))
    primal_weight = jnp.sqrt(jnp.sqrt((dual_moved + epsilon) / (primal_moved + epsilon)))
    primal_two, dual_final = iterate(primal_one, dual_one, primal_weight)
    return (primal_two, dual_final)


def solution(mesh):
    return jax.shard_map(
        per_device,
        mesh=mesh,
        in_specs=(
            P("row", "col", None, None),
            P("row", "col"),
            P("col"),
            P("row"),
            P("col"),
            P("col"),
            P("col"),
            P("col"),
            P("row"),
            P("row"),
        ),
        out_specs=(P("col"), P("row")),
        check_vma=False,
    )
```

profile of v0, /device:TPU:0, one launch (start us, length us, event | category | flops | bytes accessed | tf_op | source)
XLA Modules:
  0.0 214.4 jit_solution(8454665217977124945)
XLA Ops:
  7.2 0.0 all-reduce.6.cloned.1.call-start
  7.3 0.8 convert_bitcast_fusion.1
  8.1 0.7 compare_select_fusion
  8.8 0.1 reshape.62
  8.9 6.3 %fusion.12 = f32[8,1,48,128]{3,1,2,0:T(1,128)S(1)} fusion(bf16[8,48,128,128]{3,2,1,0:T(8,128)(2,1)} %param.10, bf16[8,128,1,1]{1,0,2,3:T(8,128)(2,1)S(1)} %convert_bitcast_fusion.1), kind=kOutput, calls=%fused_computation.31 | convolution fusion | flops 12582912 | bytes 12781568 | tf_op jit(solution)/shard_map/bsij,bi->bsj/dot_general | solution.py:44
  15.2 2.4 %scatter_custom_fusion = f32[1025,128]{1,0:T(8,128)S(1)} fusion(s32[384]{0:T(512)S(1)} %reshape.62, f32[384,128]{1,0:T(8,128)S(1)} %bitcast.47, f32[]{:T(128)} %constant.16.clone.1), kind=kCustom, calls=%fused_computation.15 | custom fusion | flops 49152 | bytes 524804 | tf_op jit(solution)/shard_map/scatter-add | solution.py:50
  17.6 0.8 slice_bitcast_fusion.1
  18.5 0.0 all-reduce.6.cloned.1.call-update
  18.5 0.0 all-reduce.8.cloned.1.call-start
  18.5 0.1 reshape.46
  18.6 0.0 copy-start.6
  18.7 0.0 copy-start.7
  18.7 74.7 %all-reduce.6.cloned.1.call-done = f32[131072]{0:T(1024)} async-done(((f32[131072]{0:T(1024)}), f32[131072]{0:T(1024)}) %all-reduce.6.cloned.1.call-update) | async-done | bytes 524304 | tf_op jit(solution)/shard_map/psum | solution.py:72
  93.4 0.0 copy-done.1
  93.4 0.0 copy-done.4
  93.4 2.0 multiply_reduce_fusion
  95.4 0.1 fusion.4
  95.5 1.4 gather_fusion
  96.9 6.4 %fusion.8 = f32[8,1,128,1]{2,1,3,0:T(1,128)S(1)} fusion(bf16[8,48,128,128]{3,2,1,0:T(8,128)(2,1)} %param.10, bf16[8,48,128,1]{2,1,0,3:T(8,128)(2,1)S(1)} %bitcast.45), kind=kOutput, calls=%fused_computation.23 | convolution fusion | flops 12582912 | bytes 12685312 | tf_op jit(solution)/shard_map/bsij,bsj->bi/dot_general | solution.py:63
  103.3 5.7 %psum.43 = f32[1024]{0:T(1024)S(1)} all-reduce(f32[1024]{0:T(1024)S(1)} %bitcast.48), channel_id=1, replica_groups=mesh['row'=8,'col'=4] {'col'}, use_global_device_ids=true, to_apply=%region_2.3 | all-reduce | flops 1024 | bytes 8192 | tf_op jit(solution)/shard_map/psum | solution.py:66
  109.0 0.7 multiply_reduce_fusion.1
  109.7 6.3 %fusion.10 = f32[8,1,48,128]{3,1,2,0:T(1,128)S(1)} fusion(bf16[8,48,128,128]{3,2,1,0:T(8,128)(2,1)} %param.10, bf16[8,128,1,1]{1,0,2,3:T(8,128)(2,1)S(1)} %convert_bitcast_fusion), kind=kOutput, calls=%fused_computation.29 | convolution fusion | flops 12582912 | bytes 12781568 | tf_op jit(solution)/shard_map/bsij,bi->bsj/dot_general | solution.py:44
  116.0 2.4 %scatter_custom_fusion.1 = f32[1025,128]{1,0:T(8,128)S(1)} fusion(s32[384]{0:T(512)S(1)} %reshape.62, f32[384,128]{1,0:T(8,128)S(1)} %bitcast.46, f32[]{:T(128)} %constant.16.clone.1), kind=kCustom, calls=%fused_computation.13 | custom fusion | flops 49152 | bytes 524804 | tf_op jit(solution)/shard_map/scatter-add | solution.py:50
  118.4 0.8 slice_bitcast_fusion
  119.3 0.0 all-reduce.8.cloned.1.call-update
  120.6 40.1 %all-reduce.2 = (f32[]{:T(128)}, f32[]{:T(128)}) all-reduce(f32[]{:T(128)S(6)} %select_n.40, f32[]{:T(128)S(6)} %select_n.41), channel_id=1, replica_groups=mesh['row'=8,'col'=4] {'row','col'}, use_global_device_ids=true, to_apply=%region_4.5 | all-reduce | flops 2 | bytes 16 | tf_op jit(solution)/shard_map/psum | solution.py:86
  162.2 29.0 %all-reduce.8.cloned.1.call-done = f32[131072]{0:T(1024)} async-done(((f32[131072]{0:T(1024)}), f32[131072]{0:T(1024)}) %all-reduce.8.cloned.1.call-update) | async-done | bytes 524304 | tf_op jit(solution)/shard_map/psum | solution.py:72
  191.3 2.1 fusion.5
  193.4 1.4 gather_fusion.1
  194.9 6.4 %fusion.6 = f32[8,1,128,1]{2,1,3,0:T(1,128)S(1)} fusion(bf16[8,48,128,128]{3,2,1,0:T(8,128)(2,1)} %param.10, bf16[8,48,128,1]{2,1,0,3:T(8,128)(2,1)S(1)} %bitcast.44), kind=kOutput, calls=%fused_computation.21 | convolution fusion | flops 12582912 | bytes 12685312 | tf_op jit(solution)/shard_map/bsij,bsj->bi/dot_general | solution.py:63
  201.3 5.7 %psum.47 = f32[1024]{0:T(1024)S(1)} all-reduce(f32[1024]{0:T(1024)S(1)} %bitcast.49), channel_id=1, replica_groups=mesh['row'=8,'col'=4] {'col'}, use_global_device_ids=true, to_apply=%region_9.10 | all-reduce | flops 1024 | bytes 8192 | tf_op jit(solution)/shard_map/psum | solution.py:66
  206.9 0.6 maximum_select_fusion.2
  (16 shorter events, 0.1 us)
Async XLA Ops:
  7.2 86.2 %copy-start.1 = (f32[131072]{0:T(1024)S(1)}, f32[131072]{0:T(1024)}, u32[]{:S(2)}) copy-start(f32[131072]{0:T(1024)} %param.16) | copy-start | bytes 1572868
  7.2 86.2 %copy-start.2 = (f32[131072]{0:T(1024)S(1)}, f32[131072]{0:T(1024)}, u32[]{:S(2)}) copy-start(f32[131072]{0:T(1024)} %param.15) | copy-start | bytes 1572868
  7.2 86.2 %copy-start.3 = (f32[131072]{0:T(1024)S(1)}, f32[131072]{0:T(1024)}, u32[]{:S(2)}) copy-start(f32[131072]{0:T(1024)} %param.14) | copy-start | bytes 1572868
  7.2 86.2 %copy-start = (f32[131072]{0:T(1024)S(1)}, f32[131072]{0:T(1024)}, u32[]{:S(2)}) copy-start(f32[131072]{0:T(1024)} %param.12) | copy-start | bytes 1572868
  7.2 86.2 %copy-start.4 = (s32[131072]{0:T(1024)S(1)}, s32[131072]{0:T(1024)}, u32[]{:S(2)}) copy-start(s32[131072]{0:T(1024)} %param.17) | copy-start | bytes 1572868
  7.2 86.1 %all-reduce.6.cloned.1.call-start = ((), (), s32[]{:S(2)}) async-start(), calls=%async_computation | async-start | bytes 1048576 | tf_op jit(solution)/shard_map/psum | solution.py:72
  18.5 172.8 %all-reduce.8.cloned.1.call-start = ((), (), s32[]{:S(2)}) async-start(), calls=%async_computation.1 | async-start | bytes 1048576 | tf_op jit(solution)/shard_map/psum | solution.py:72
  18.6 90.3 %copy-start.5 = (f32[1024]{0:T(1024)S(1)}, f32[1024]{0:T(1024)}, u32[]{:S(2)}) copy-start(f32[1024]{0:T(1024)} %param.13) | copy-start | bytes 12292
  18.6 90.3 %copy-start.6 = (f32[1024]{0:T(1024)S(1)}, f32[1024]{0:T(1024)}, u32[]{:S(2)}) copy-start(f32[1024]{0:T(1024)} %param.18) | copy-start | bytes 12292
  18.7 90.3 %copy-start.7 = (s32[1024]{0:T(1024)S(1)}, s32[1024]{0:T(1024)}, u32[]{:S(2)}) copy-start(s32[1024]{0:T(1024)} %param.19) | copy-start | bytes 12292
Sparse Core Ops, SparseCore 0:
  18.6 74.6 all-reduce.5
  119.4 71.8 all-reduce.7
where the time goes:
time: 215 us; the launch traced here: 214 us
  waiting for transfers between devices  104 us (48%)
  blocking collectives  51.4 us (24%)
  matrix products  25.4 us (12%)
  between operations  17 us (8%)
  other arithmetic  11.9 us (6%)
  local copies, waits for them, and re-layouts  4.79 us (2%)
    psum x2, waiting for transfers between devices, iterate(): col_product = lax.psum(partial_value, 'row')  104 us
    psum x1, blocking collectives, per_device(): lax.psum((primal_share, dual_share), ('row', 'col'))  40.1 us
    dot_general x2, matrix products, forward_total(): jnp.einsum('bsij,bsj->bi', tile_values, picked, preferred_element_type=jn...  12.8 us
    dot_general x2, matrix products, transpose_partial(): jnp.einsum('bsij,bi->bsj', tile_values, dual_half.reshape(band_count, til...  12.6 us
    psum x2, blocking collectives, forward_total(): return lax.psum(partial_value, 'col')  11.3 us
    scatter-add x2, other arithmetic, transpose_partial(): jax.ops.segment_sum(contrib.reshape(band_count * slot_count, tile_width),...  4.89 us
  transfers between devices with their start and end apart: 2, of which 2 were waited for; matrix products, arithmetic and copies ran while one was open for 0% of the time, Pallas kernels for 0%

commit v1 on v0

v1 whole, which is shorter than its diff:
```python
import functools

import jax
import jax.numpy as jnp
from jax import lax
from jax.experimental import pallas as pl
from jax.experimental.pallas import tpu as pltpu
from jax.sharding import PartitionSpec as P

step_size = 0.8
epsilon = 1e-06
OUTER = 4
GROUP = 16
CHUNKS = 2
MESH_ID = pl.DeviceIdType.MESH


def project_primal(vector, lower_bound, upper_bound, var_kinds):
    raised = jnp.where(var_kinds >= 1, jnp.maximum(vector, lower_bound), vector)
    return jnp.where(var_kinds == 2, jnp.minimum(raised, upper_bound), raised)


def project_dual(vector, row_kinds):
    return jnp.where(row_kinds == 1, jnp.maximum(vector, 0.0), vector)


def kernel(
    rows, cols, bands, slots, width, blocks,
    tiles_hbm, ids_row, ids_col, primal_hbm, cost_hbm, lower_hbm, upper_hbm, kinds_hbm,
    dual_ref, right_ref, row_kinds_ref,
    primal_out, dual_out,
    tiles, primal, cost, lower, upper, kinds, result,
    hot, hot_own, xbar, picked, contrib, ids_all, partial, moved_dual,
    tile_sem, in_sem, out_sem,
    own_send, fwd_send, con_recv, ids_send, ids_recv, par_send, par_recv, mov_send, mov_recv,
):
    inner = rows // OUTER
    local = bands * slots
    per_chunk = local // CHUNKS
    row = lax.axis_index("row")
    col = lax.axis_index("col")
    outer_at = row // inner
    inner_at = lax.rem(row, inner)

    def place(dz, dy):
        return lax.rem(outer_at + dz + OUTER, OUTER) * inner + lax.rem(inner_at + dy + inner, inner)

    tile_copies = [
        pltpu.make_async_copy(tiles_hbm.at[b], tiles.at[b], tile_sem.at[b]) for b in range(bands)
    ]
    for copy in tile_copies:
        copy.start()
    in_copies = [
        pltpu.make_async_copy(src, dst, in_sem.at[i])
        for i, (src, dst) in enumerate(
            [(primal_hbm, primal), (cost_hbm, cost), (lower_hbm, lower), (upper_hbm, upper), (kinds_hbm, kinds)]
        )
    ]
    for copy in in_copies:
        copy.start()

    barrier = pltpu.get_barrier_semaphore()
    for d in range(1, rows):
        pl.semaphore_signal(barrier, 1, device_id={"row": lax.rem(row + d, rows)}, device_id_type=MESH_ID)
    for d in range(1, cols):
        pl.semaphore_signal(barrier, 1, device_id={"col": lax.rem(col + d, cols)}, device_id_type=MESH_ID)

    pending = []

    def remote(src, dst, send, recv, target):
        copy = pltpu.make_async_remote_copy(
            src_ref=src, dst_ref=dst, send_sem=send, recv_sem=recv,
            device_id=target, device_id_type=MESH_ID,
        )
        copy.start()
        pending.append(copy)

    def await_recv(ref, recv):
        pltpu.make_async_copy(ref, ref, recv).wait()

    lane_block = lax.broadcasted_iota(jnp.int32, (GROUP, GROUP * width), 1) // width
    row_at = lax.broadcasted_iota(jnp.int32, (GROUP, GROUP * width), 0)
    diagonal = lane_block == row_at

    def transposed(it, source, first, count):
        def band(b, carry):
            line = source[pl.ds(b, 1), :]
            wide = jnp.concatenate([jnp.broadcast_to(line, (GROUP, width))] * GROUP, axis=1)
            left = jnp.where(diagonal, wide, 0.0).astype(jnp.bfloat16)
            for g in range(slots // GROUP):
                right = tiles[b, g * GROUP:(g + 1) * GROUP].reshape(GROUP * width, width)
                value = jnp.dot(left, right, preferred_element_type=jnp.float32)
                at = pl.multiple_of(b * slots + g * GROUP, GROUP)
                high = value.astype(jnp.bfloat16)
                low = (value - high.astype(jnp.float32)).astype(jnp.bfloat16)
                contrib[it, row, pl.ds(at, GROUP), :width] = high
                contrib[it, row, pl.ds(at, GROUP), width:] = low
            return carry

        lax.fori_loop(first, first + count, band, 0, unroll=True)

    def chunk_ref(it, src, c):
        return contrib.at[it, src, pl.ds(c * per_chunk, per_chunk), :]

    def send_chunk(it, c):
        for dy in range(1, inner):
            remote(chunk_ref(it, row, c), chunk_ref(it, row, c), own_send.at[it, 0, dy, c],
                   con_recv.at[it, 0, dy, c], {"row": place(0, dy)})
        for dz in range(1, OUTER):
            remote(chunk_ref(it, row, c), chunk_ref(it, row, c), own_send.at[it, dz, 0, c],
                   con_recv.at[it, dz, 0, c], {"row": place(dz, 0)})

    def forward_chunks(it, meanwhile):
        for dz in range(1, OUTER):
            src = place(-dz, 0)
            for c in range(CHUNKS):
                await_recv(chunk_ref(it, src, c), con_recv.at[it, dz, 0, c])
                for dy in range(1, inner):
                    remote(chunk_ref(it, src, c), chunk_ref(it, src, c), fwd_send.at[it, dz, dy, c],
                           con_recv.at[it, dz, dy, c], {"row": place(0, dy)})
            meanwhile(dz)

    def gather_rest(it):
        for dz in range(OUTER):
            for dy in range(1, inner):
                for c in range(CHUNKS):
                    await_recv(chunk_ref(it, place(-dz, -dy), c), con_recv.at[it, dz, dy, c])

    def build_hot(src):
        line = ids_all[pl.ds(src, 1), 0, :]

        def part(i, carry):
            at = pl.multiple_of(i * 128, 128)
            index = lax.broadcasted_iota(jnp.int32, (128, local), 0) + at
            hot[src, pl.ds(at, 128), :] = jnp.where(index == line, 1.0, 0.0).astype(jnp.bfloat16)
            return carry

        lax.fori_loop(0, blocks // 128, part, 0)

    def primal_update(it, primal_step):
        size = 128

        def part(i, moved):
            at = pl.multiple_of(i * size, size)
            here = pl.ds(at, size)
            product = jnp.zeros((size, 2 * width), jnp.float32)
            for src in range(rows):
                product = product + jnp.dot(hot[src, here, :], contrib[it, src], preferred_element_type=jnp.float32)
            product = product[:, :width] + product[:, width:]
            old = primal[here, :] if it == 0 else result[here, :]
            new = project_primal(
                old - primal_step * (cost[here, :] - product), lower[here, :], upper[here, :], kinds[here, :]
            )
            result[here, :] = new
            xbar[here, :] = (2.0 * new - old).astype(jnp.bfloat16)
            square = (new - old) ** 2
            return moved + jnp.sum(square.reshape(size // 8, 8, width), axis=0)

        return lax.fori_loop(0, blocks // size, part, jnp.zeros((8, width), jnp.float32), unroll=2)

    def forward(it):
        picked[...] = jnp.dot(hot_own[...], xbar[...], preferred_element_type=jnp.float32).astype(jnp.bfloat16)

        def band(b, carry):
            total = jnp.zeros((GROUP, GROUP * width), jnp.float32)
            for g in range(slots // GROUP):
                right = tiles[b, g * GROUP:(g + 1) * GROUP].reshape(GROUP * width, width)
                at = pl.multiple_of(b * slots + g * GROUP, GROUP)
                total = total + lax.dot_general(
                    picked[pl.ds(at, GROUP), :], right, (((1,), (1,)), ((), ())),
                    preferred_element_type=jnp.float32,
                )
            total = jnp.where(diagonal, total, 0.0)
            lanes = total[:, :width]
            for k in range(1, GROUP):
                lanes = lanes + total[:, k * width:(k + 1) * width]
            partial[it, col, pl.ds(b, 1), :] = jnp.sum(lanes, axis=0, keepdims=True)
            return carry

        lax.fori_loop(0, bands, band, 0, unroll=True)

    def exchange_partials(it):
        for d in range(1, cols):
            remote(partial.at[it, col], partial.at[it, col], par_send.at[it, d], par_recv.at[it, d],
                   {"col": lax.rem(col + d, cols)})
        for d in range(1, cols):
            await_recv(partial.at[it, lax.rem(col + cols - d, cols)], par_recv.at[it, d])
        total = partial[it, 0]
        for c in range(1, cols):
            total = total + partial[it, c]
        return total

    ids_all[row] = ids_row[...]

    per_bands = bands // CHUNKS
    for c in range(CHUNKS):
        for b in range(c * per_bands, (c + 1) * per_bands):
            tile_copies[b].wait()
        transposed(0, dual_ref, c * per_bands, per_bands)
        if c == 0:
            pl.semaphore_wait(barrier, rows + cols - 2)
        send_chunk(0, c)
    for d in range(1, rows):
        remote(ids_all.at[row], ids_all.at[row], ids_send.at[d], ids_recv.at[d], {"row": lax.rem(row + d, rows)})
    index = lax.broadcasted_iota(jnp.int32, (local, blocks), 1)
    hot_own[...] = jnp.where(index == ids_col[...], 1.0, 0.0).astype(jnp.bfloat16)
    build_hot(row)
    for copy in in_copies:
        copy.wait()
    for d in range(1, rows):
        await_recv(ids_all.at[lax.rem(row + rows - d, rows)], ids_recv.at[d])

    def build_hots(dz):
        for dy in range(inner):
            build_hot(place(-dz, -dy))

    forward_chunks(0, build_hots)
    for dy in range(1, inner):
        build_hot(place(0, -dy))
    gather_rest(0)
    moved_primal = primal_update(0, step_size)
    partial[0, col, 8:16, :] = moved_primal
    forward(0)
    total = exchange_partials(0)
    dual = dual_ref[...]
    dual_one = project_dual(dual + step_size * (right_ref[...] - total[:bands]), row_kinds_ref[...])
    dual_out[...] = dual_one
    moved_dual[row] = (dual_one - dual) ** 2
    moved_primal = jnp.sum(total[8:16], keepdims=True)

    for d in range(1, rows):
        remote(moved_dual.at[row], moved_dual.at[row], mov_send.at[d], mov_recv.at[d],
               {"row": lax.rem(row + d, rows)})
    for c in range(CHUNKS):
        transposed(1, dual_out, c * per_bands, per_bands)
        send_chunk(1, c)
    for d in range(1, rows):
        await_recv(moved_dual.at[lax.rem(row + rows - d, rows)], mov_recv.at[d])
    squares = moved_dual[0]
    for r in range(1, rows):
        squares = squares + moved_dual[r]
    weight = jnp.sqrt(jnp.sqrt((jnp.sum(squares, keepdims=True) + epsilon) / (moved_primal + epsilon)))
    forward_chunks(1, lambda dz: None)
    gather_rest(1)
    primal_update(1, step_size / weight)
    out_copy = pltpu.make_async_copy(result, primal_out, out_sem)
    out_copy.start()
    partial[1, col, 8:16, :] = jnp.zeros((8, width), jnp.float32)
    forward(1)
    total = exchange_partials(1)
    dual_out[...] = project_dual(
        dual_one + (step_size * weight) * (right_ref[...] - total[:bands]), row_kinds_ref[...]
    )
    for copy in pending:
        copy.wait_send()
    out_copy.wait()


def per_device(
    rows, cols,
    tile_values, block_cols, primal_start, dual_start, cost_vector,
    lower_bound, upper_bound, var_kinds, right_side, row_kinds,
):
    bands, slots, width, _ = tile_values.shape
    blocks = primal_start.shape[0] // width
    local = bands * slots
    inner = rows // OUTER
    ids = block_cols - lax.axis_index("col") * blocks
    vmem = pl.BlockSpec(memory_space=pltpu.VMEM)
    hbm = pl.BlockSpec(memory_space=pl.ANY)
    dma = pltpu.SemaphoreType.DMA
    tall = (blocks, width)
    primal_final, dual_final = pl.pallas_call(
        functools.partial(kernel, rows, cols, bands, slots, width, blocks),
        out_shape=(
            jax.ShapeDtypeStruct(tall, jnp.float32),
            jax.ShapeDtypeStruct((bands, width), jnp.float32),
        ),
        in_specs=[hbm, vmem, vmem] + [hbm] * 5 + [vmem] * 3,
        out_specs=(hbm, vmem),
        scratch_shapes=[
            pltpu.VMEM((bands, slots, width, width), jnp.bfloat16),
            pltpu.VMEM(tall, jnp.float32),
            pltpu.VMEM(tall, jnp.float32),
            pltpu.VMEM(tall, jnp.float32),
            pltpu.VMEM(tall, jnp.float32),
            pltpu.VMEM(tall, jnp.int32),
            pltpu.VMEM(tall, jnp.float32),
            pltpu.VMEM((rows, blocks, local), jnp.bfloat16),
            pltpu.VMEM((local, blocks), jnp.bfloat16),
            pltpu.VMEM(tall, jnp.bfloat16),
            pltpu.VMEM((local, width), jnp.bfloat16),
            pltpu.VMEM((2, rows, local, 2 * width), jnp.bfloat16),
            pltpu.VMEM((rows, 1, local), jnp.int32),
            pltpu.VMEM((2, cols, 16, width), jnp.float32),
            pltpu.VMEM((rows, bands, width), jnp.float32),
            dma((bands,)),
            dma((5,)),
            dma,
            dma((2, OUTER, inner, CHUNKS)),
            dma((2, OUTER, inner, CHUNKS)),
            dma((2, OUTER, inner, CHUNKS)),
            dma((rows,)),
            dma((rows,)),
            dma((2, cols)),
            dma((2, cols)),
            dma((rows,)),
            dma((rows,)),
        ],
        compiler_params=pltpu.CompilerParams(
            collective_id=0, has_side_effects=True, vmem_limit_bytes=56 * 1024 * 1024
        ),
    )(
        tile_values,
        ids.reshape(1, local),
        ids.reshape(local, 1),
        primal_start.reshape(tall),
        cost_vector.reshape(tall),
        lower_bound.reshape(tall),
        upper_bound.reshape(tall),
        var_kinds.reshape(tall),
        dual_start.reshape(bands, width),
        right_side.reshape(bands, width),
        row_kinds.reshape(bands, width),
    )
    return primal_final.reshape(-1), dual_final.reshape(-1)


def solution(mesh):
    return jax.shard_map(
        functools.partial(per_device, mesh.shape["row"], mesh.shape["col"]),
        mesh=mesh,
        in_specs=(
            P("row", "col", None, None),
            P("row", "col"),
            P("col"),
            P("row"),
            P("col"),
            P("col"),
            P("col"),
            P("col"),
            P("row"),
            P("row"),
        ),
        out_specs=(P("col"), P("row")),
        check_vma=False,
    )
```

time: 215 us -> 95.3 us (0.44)
  the two profiles are of different devices: /device:TPU:0 before, /device:TPU:17 now
where the time goes in v1:
time: 95.3 us; the launch traced here: 95.1 us
  Pallas kernels  89.2 us (94%)
  local copies, waits for them, and re-layouts  4.57 us (5%)
    pallas_call x1, Pallas kernels, per_device(): pl.pallas_call(functools.partial(kernel, rows, cols, bands, slots, width,...  89.2 us
    unnamed x2, local copies, waits for them, and re-layouts  3.13 us

profile of v1, /device:TPU:17, one launch (start us, length us, event | category | flops | bytes accessed | tf_op | source)
XLA Modules:
  0.0 95.1 jit_solution(18172138438555779170)
XLA Ops:
  0.6 0.7 broadcast_subtract_fusion
  1.3 0.6 reshape.40.ids_row
  2.0 0.8 reshape.52.ids_col
  2.8 89.2 %shard_map.113 = (f32[1024,128]{1,0:T(8,128)}, f32[8,128]{1,0:T(8,128)}) custom-call(bf16[8,48,128,128]{3,2,1,0:T(8,128)(2,1)} %tiles_hbm.1, s32[1,384]{1,0:T(1,128)} %reshape.40.ids_row, s32[384,1]{1,0:T(8,128)} %reshape.52.ids_col, f32[1024,128]{1,0:T(8,128)} %bitcast.10, f32[1024,128]{1,0:T(8,128)} %bitcast.11, f32[1024,128]{1,0:T(8,128)} %bitcast.12, ...), custom_call_target="tpu_custom_call" | custom-call | tf_op jit(solution)/shard_map/pallas_call | solution.py:273
  92.0 1.9 %copy.15 = f32[131072]{0:T(1024)} copy(f32[131072]{0:T(1024)} %bitcast.15) | data formatting | bytes 1048576
  93.8 1.3 %copy.16 = f32[1024]{0:T(1024)} copy(f32[1024]{0:T(1024)} %bitcast.19) | data formatting | bytes 8192

commit v2 on v1

v2 whole, which is shorter than its diff:
```python
import functools

import jax
import jax.numpy as jnp
from jax import lax
from jax.experimental import pallas as pl
from jax.experimental.pallas import tpu as pltpu
from jax.sharding import PartitionSpec as P

step_size = 0.8
epsilon = 1e-06
OUTER = 4
GROUP = 16
CHUNKS = 2
MESH_ID = pl.DeviceIdType.MESH


def project_primal(vector, lower_bound, upper_bound, var_kinds):
    raised = jnp.where(var_kinds >= 1, jnp.maximum(vector, lower_bound), vector)
    return jnp.where(var_kinds == 2, jnp.minimum(raised, upper_bound), raised)


def project_dual(vector, row_kinds):
    return jnp.where(row_kinds == 1, jnp.maximum(vector, 0.0), vector)


def kernel(
    rows, cols, bands, slots, width, blocks,
    tiles_hbm, ids_row, ids_col, primal_hbm, cost_hbm, lower_hbm, upper_hbm, kinds_hbm,
    dual_ref, right_ref, row_kinds_ref,
    primal_out, dual_out,
    tiles, primal, cost, lower, upper, kinds, mine, result,
    hot, hot_own, spread, picked, contrib, ids_all, stage, arrived, partial, moved,
    tile_sem, in_sem, out_sem,
    con_send, con_recv, sum_send, sum_recv, own_send, fwd_send, spr_recv, ids_send, ids_recv, par_send, par_recv, mov_send, mov_recv,
):
    inner = rows // OUTER
    local = bands * slots
    per_chunk = local // CHUNKS
    row = lax.axis_index("row")
    col = lax.axis_index("col")
    outer_at = row // inner
    inner_at = lax.rem(row, inner)
    part_rows = blocks // inner
    own_rows = blocks // rows

    def owned(outer_place, inner_place):
        return pl.ds(pl.multiple_of(inner_place * part_rows + outer_place * own_rows, own_rows), own_rows)

    own = owned(outer_at, inner_at)

    def place(dz, dy):
        return lax.rem(outer_at + dz + OUTER, OUTER) * inner + lax.rem(inner_at + dy + inner, inner)

    tile_copies = [
        pltpu.make_async_copy(tiles_hbm.at[b], tiles.at[b], tile_sem.at[b]) for b in range(bands)
    ]
    for copy in tile_copies:
        copy.start()
    in_copies = [
        pltpu.make_async_copy(src.at[own, :], dst, in_sem.at[i])
        for i, (src, dst) in enumerate(
            [(primal_hbm, primal), (cost_hbm, cost), (lower_hbm, lower), (upper_hbm, upper), (kinds_hbm, kinds)]
        )
    ]
    for copy in in_copies:
        copy.start()

    barrier = pltpu.get_barrier_semaphore()
    for d in range(1, rows):
        pl.semaphore_signal(barrier, 1, device_id={"row": lax.rem(row + d, rows)}, device_id_type=MESH_ID)
    for d in range(1, cols):
        pl.semaphore_signal(barrier, 1, device_id={"col": lax.rem(col + d, cols)}, device_id_type=MESH_ID)

    pending = []

    def remote(src, dst, send, recv, target):
        copy = pltpu.make_async_remote_copy(
            src_ref=src, dst_ref=dst, send_sem=send, recv_sem=recv,
            device_id=target, device_id_type=MESH_ID,
        )
        copy.start()
        pending.append(copy)

    def await_recv(ref, recv):
        pltpu.make_async_copy(ref, ref, recv).wait()

    lane_block = lax.broadcasted_iota(jnp.int32, (GROUP, GROUP * width), 1) // width
    row_at = lax.broadcasted_iota(jnp.int32, (GROUP, GROUP * width), 0)
    diagonal = lane_block == row_at

    def transposed(it, source, first, count):
        def band(b, carry):
            line = source[pl.ds(b, 1), :]
            wide = jnp.concatenate([jnp.broadcast_to(line, (GROUP, width))] * GROUP, axis=1)
            left = jnp.where(diagonal, wide, 0.0).astype(jnp.bfloat16)
            for g in range(slots // GROUP):
                right = tiles[b, g * GROUP:(g + 1) * GROUP].reshape(GROUP * width, width)
                value = jnp.dot(left, right, preferred_element_type=jnp.float32)
                at = pl.multiple_of(b * slots + g * GROUP, GROUP)
                high = value.astype(jnp.bfloat16)
                low = (value - high.astype(jnp.float32)).astype(jnp.bfloat16)
                contrib[it, inner_at, pl.ds(at, GROUP), :width] = high
                contrib[it, inner_at, pl.ds(at, GROUP), width:] = low
            return carry

        lax.fori_loop(first, first + count, band, 0, unroll=True)

    def chunk_ref(it, src, c):
        return contrib.at[it, src, pl.ds(c * per_chunk, per_chunk), :]

    def send_chunk(it, c):
        for dy in range(1, inner):
            remote(chunk_ref(it, inner_at, c), chunk_ref(it, inner_at, c), con_send.at[it, dy, c],
                   con_recv.at[it, dy, c], {"row": place(0, dy)})

    def spread_start(k):
        for dz in range(1, OUTER):
            remote(spread.at[k, own, :], spread.at[k, own, :], own_send.at[k, dz, 0],
                   spr_recv.at[k, dz, 0], {"row": place(dz, 0)})
        for dy in range(1, inner):
            remote(spread.at[k, own, :], spread.at[k, own, :], own_send.at[k, 0, dy],
                   spr_recv.at[k, 0, dy], {"row": place(0, dy)})

    def spread_finish(k):
        for dz in range(1, OUTER):
            here = spread.at[k, owned(lax.rem(outer_at + OUTER - dz, OUTER), inner_at), :]
            await_recv(here, spr_recv.at[k, dz, 0])
            for dy in range(1, inner):
                remote(here, here, fwd_send.at[k, dz, dy], spr_recv.at[k, dz, dy], {"row": place(0, dy)})
        for dz in range(OUTER):
            for dy in range(1, inner):
                there = owned(lax.rem(outer_at + OUTER - dz, OUTER), lax.rem(inner_at + inner - dy, inner))
                await_recv(spread.at[k, there, :], spr_recv.at[k, dz, dy])

    def build_hot(src):
        line = ids_all[src] - inner_at * part_rows

        def part(i, carry):
            at = pl.multiple_of(i * 64, 64)
            index = lax.broadcasted_iota(jnp.int32, (64, local), 0) + at
            hot[src, pl.ds(at, 64), :] = jnp.where(index == line, 1.0, 0.0).astype(jnp.bfloat16)
            return carry

        lax.fori_loop(0, part_rows // 64, part, 0)

    def reduce_to_owner(it):
        for dy in range(1, inner):
            for c in range(CHUNKS):
                await_recv(chunk_ref(it, lax.rem(inner_at + inner - dy, inner), c), con_recv.at[it, dy, c])
        for dz in list(range(1, OUTER)) + [0]:
            target = lax.rem(outer_at + dz, OUTER)
            at = pl.ds(pl.multiple_of(target * own_rows, own_rows), own_rows)
            product = jnp.zeros((own_rows, 2 * width), jnp.float32)
            for src in range(inner):
                product = product + jnp.dot(hot[src, at, :], contrib[it, src], preferred_element_type=jnp.float32)
            product = product[:, :width] + product[:, width:]
            if dz == 0:
                arrived[it, outer_at] = product
            else:
                stage[it, dz] = product
                remote(stage.at[it, dz], arrived.at[it, outer_at], sum_send.at[it, dz], sum_recv.at[it, dz],
                       {"row": place(dz, 0)})
        for dz in range(1, OUTER):
            await_recv(arrived.at[it, lax.rem(outer_at + OUTER - dz, OUTER)], sum_recv.at[it, dz])
        total = arrived[it, 0]
        for z in range(1, OUTER):
            total = total + arrived[it, z]
        return total

    def primal_update(it, primal_step):
        product = reduce_to_owner(it)
        old = primal[...] if it == 0 else mine[...]
        new = project_primal(old - primal_step * (cost[...] - product), lower[...], upper[...], kinds[...])
        spread[it, own, :] = (2.0 * new - old).astype(jnp.bfloat16)
        spread_start(it)
        if it == 0:
            mine[...] = new
        else:
            spread[2, own, :] = new.astype(jnp.bfloat16)
            spread_start(2)
        return jnp.sum(((new - old) ** 2).reshape(own_rows // 8, 8, width), axis=0)

    def forward(it):
        picked[...] = jnp.dot(hot_own[...], spread[it], preferred_element_type=jnp.float32).astype(jnp.bfloat16)

        def band(b, carry):
            total = jnp.zeros((GROUP, GROUP * width), jnp.float32)
            for g in range(slots // GROUP):
                right = tiles[b, g * GROUP:(g + 1) * GROUP].reshape(GROUP * width, width)
                at = pl.multiple_of(b * slots + g * GROUP, GROUP)
                total = total + lax.dot_general(
                    picked[pl.ds(at, GROUP), :], right, (((1,), (1,)), ((), ())),
                    preferred_element_type=jnp.float32,
                )
            total = jnp.where(diagonal, total, 0.0)
            lanes = total[:, :width]
            for k in range(1, GROUP):
                lanes = lanes + total[:, k * width:(k + 1) * width]
            partial[it, col, pl.ds(b, 1), :] = jnp.sum(lanes, axis=0, keepdims=True)
            return carry

        lax.fori_loop(0, bands, band, 0, unroll=True)

    def send_partials(it):
        for d in range(1, cols):
            remote(partial.at[it, col], partial.at[it, col], par_send.at[it, d], par_recv.at[it, d],
                   {"col": lax.rem(col + d, cols)})

    def sum_partials(it):
        for d in range(1, cols):
            await_recv(partial.at[it, lax.rem(col + cols - d, cols)], par_recv.at[it, d])
        total = partial[it, 0]
        for c in range(1, cols):
            total = total + partial[it, c]
        return total

    ids_all[inner_at] = ids_row[...]

    pl.semaphore_wait(barrier, rows + cols - 2)
    for d in range(1, inner):
        remote(ids_all.at[inner_at], ids_all.at[inner_at], ids_send.at[d], ids_recv.at[d], {"row": place(0, d)})
    per_bands = bands // CHUNKS
    for c in range(CHUNKS):
        for b in range(c * per_bands, (c + 1) * per_bands):
            tile_copies[b].wait()
        transposed(0, dual_ref, c * per_bands, per_bands)
        send_chunk(0, c)
    for d in range(1, inner):
        await_recv(ids_all.at[lax.rem(inner_at + inner - d, inner)], ids_recv.at[d])
    for src in range(inner):
        build_hot(src)
    index = lax.broadcasted_iota(jnp.int32, (local, blocks), 1)
    hot_own[...] = jnp.where(index == ids_col[...], 1.0, 0.0).astype(jnp.bfloat16)
    for copy in in_copies:
        copy.wait()
    partial[0, col, 8:16, :] = primal_update(0, step_size)
    spread_finish(0)
    forward(0)
    send_partials(0)
    total = sum_partials(0)
    dual = dual_ref[...]
    dual_one = project_dual(dual + step_size * (right_ref[...] - total[:bands]), row_kinds_ref[...])
    dual_out[...] = dual_one
    moved[row, :bands, :] = (dual_one - dual) ** 2
    moved[row, bands:, :] = total[8:16]

    for c in range(CHUNKS):
        transposed(1, dual_out, c * per_bands, per_bands)
        send_chunk(1, c)
        if c == 0:
            for d in range(1, rows):
                remote(moved.at[row], moved.at[row], mov_send.at[d], mov_recv.at[d],
                       {"row": lax.rem(row + d, rows)})
    for d in range(1, rows):
        await_recv(moved.at[lax.rem(row + rows - d, rows)], mov_recv.at[d])
    squares = moved[0]
    for r in range(1, rows):
        squares = squares + moved[r]
    dual_moved = jnp.sum(squares[:bands], keepdims=True)
    primal_moved = jnp.sum(squares[bands:], keepdims=True)
    weight = jnp.sqrt(jnp.sqrt((dual_moved + epsilon) / (primal_moved + epsilon)))
    primal_update(1, step_size / weight)
    partial[1, col, 8:16, :] = jnp.zeros((8, width), jnp.float32)
    spread_finish(1)
    forward(1)
    send_partials(1)
    spread_finish(2)
    result[...] = spread[2].astype(jnp.float32)
    out_copy = pltpu.make_async_copy(result, primal_out, out_sem)
    out_copy.start()
    total = sum_partials(1)
    dual_out[...] = project_dual(
        dual_one + (step_size * weight) * (right_ref[...] - total[:bands]), row_kinds_ref[...]
    )
    for copy in pending:
        copy.wait_send()
    out_copy.wait()


def per_device(
    rows, cols,
    tile_values, block_cols, primal_start, dual_start, cost_vector,
    lower_bound, upper_bound, var_kinds, right_side, row_kinds,
):
    bands, slots, width, _ = tile_values.shape
    blocks = primal_start.shape[0] // width
    local = bands * slots
    inner = rows // OUTER
    ids = block_cols - lax.axis_index("col") * blocks
    vmem = pl.BlockSpec(memory_space=pltpu.VMEM)
    hbm = pl.BlockSpec(memory_space=pl.ANY)
    dma = pltpu.SemaphoreType.DMA
    tall = (blocks, width)
    short = (blocks // rows, width)
    primal_final, dual_final = pl.pallas_call(
        functools.partial(kernel, rows, cols, bands, slots, width, blocks),
        out_shape=(
            jax.ShapeDtypeStruct(tall, jnp.float32),
            jax.ShapeDtypeStruct((bands, width), jnp.float32),
        ),
        in_specs=[hbm, vmem, vmem] + [hbm] * 5 + [vmem] * 3,
        out_specs=(hbm, vmem),
        scratch_shapes=[
            pltpu.VMEM((bands, slots, width, width), jnp.bfloat16),
            pltpu.VMEM(short, jnp.float32),
            pltpu.VMEM(short, jnp.float32),
            pltpu.VMEM(short, jnp.float32),
            pltpu.VMEM(short, jnp.float32),
            pltpu.VMEM(short, jnp.int32),
            pltpu.VMEM(short, jnp.float32),
            pltpu.VMEM(tall, jnp.float32),
            pltpu.VMEM((inner, blocks // inner, local), jnp.bfloat16),
            pltpu.VMEM((local, blocks), jnp.bfloat16),
            pltpu.VMEM((3,) + tall, jnp.bfloat16),
            pltpu.VMEM((local, width), jnp.bfloat16),
            pltpu.VMEM((2, inner, local, 2 * width), jnp.bfloat16),
            pltpu.VMEM((inner, 1, local), jnp.int32),
            pltpu.VMEM((2, OUTER) + short, jnp.float32),
            pltpu.VMEM((2, OUTER) + short, jnp.float32),
            pltpu.VMEM((2, cols, 16, width), jnp.float32),
            pltpu.VMEM((rows, bands + 8, width), jnp.float32),
            dma((bands,)),
            dma((5,)),
            dma,
            dma((2, inner, CHUNKS)),
            dma((2, inner, CHUNKS)),
            dma((2, OUTER)),
            dma((2, OUTER)),
            dma((3, OUTER, inner)),
            dma((3, OUTER, inner)),
            dma((3, OUTER, inner)),
            dma((inner,)),
            dma((inner,)),
            dma((2, cols)),
            dma((2, cols)),
            dma((rows,)),
            dma((rows,)),
        ],
        compiler_params=pltpu.CompilerParams(
            collective_id=0, has_side_effects=True, vmem_limit_bytes=56 * 1024 * 1024
        ),
    )(
        tile_values,
        ids.reshape(1, local),
        ids.reshape(local, 1),
        primal_start.reshape(tall),
        cost_vector.reshape(tall),
        lower_bound.reshape(tall),
        upper_bound.reshape(tall),
        var_kinds.reshape(tall),
        dual_start.reshape(bands, width),
        right_side.reshape(bands, width),
        row_kinds.reshape(bands, width),
    )
    return primal_final.reshape(-1), dual_final.reshape(-1)


def solution(mesh):
    return jax.shard_map(
        functools.partial(per_device, mesh.shape["row"], mesh.shape["col"]),
        mesh=mesh,
        in_specs=(
            P("row", "col", None, None),
            P("row", "col"),
            P("col"),
            P("row"),
            P("col"),
            P("col"),
            P("col"),
            P("col"),
            P("row"),
            P("row"),
        ),
        out_specs=(P("col"), P("row")),
        check_vma=False,
    )
```

time: 95.3 us -> 75.3 us (0.79)
  the two profiles are of different devices: /device:TPU:17 before, /device:TPU:0 now
where the time goes in v2:
time: 75.3 us; the launch traced here: 75.1 us
  Pallas kernels  69.2 us (92%)
  local copies, waits for them, and re-layouts  4.57 us (6%)
    pallas_call x1, Pallas kernels, per_device(): pl.pallas_call(functools.partial(kernel, rows, cols, bands, slots, width,...  69.2 us
    unnamed x2, local copies, waits for them, and re-layouts  3.13 us

profile of v2, /device:TPU:0, one launch (start us, length us, event | category | flops | bytes accessed | tf_op | source)
XLA Modules:
  0.0 75.1 jit_solution(4470032123217854834)
XLA Ops:
  0.6 0.7 broadcast_subtract_fusion
  1.3 0.6 reshape.40.ids_row
  2.0 0.8 %reshape.52.ids_col = s32[384,1]{1,0:T(8,128)} reshape(s32[8,48]{1,0:T(8,128)S(1)} %broadcast_subtract_fusion) | data formatting | bytes 3072 | tf_op jit(solution)/shard_map/reshape | solution.py:346
  2.8 69.2 %shard_map.113 = (f32[1024,128]{1,0:T(8,128)}, f32[8,128]{1,0:T(8,128)}) custom-call(bf16[8,48,128,128]{3,2,1,0:T(8,128)(2,1)} %tiles_hbm.1, s32[1,384]{1,0:T(1,128)} %reshape.40.ids_row, s32[384,1]{1,0:T(8,128)} %reshape.52.ids_col, f32[1024,128]{1,0:T(8,128)} %bitcast.10, f32[1024,128]{1,0:T(8,128)} %bitcast.11, f32[1024,128]{1,0:T(8,128)} %bitcast.12, ...), custom_call_target="tpu_custom_call" | custom-call | tf_op jit(solution)/shard_map/pallas_call | solution.py:296
  71.9 1.9 %copy.15 = f32[131072]{0:T(1024)} copy(f32[131072]{0:T(1024)} %bitcast.15) | data formatting | bytes 1048576
  73.8 1.3 %copy.16 = f32[1024]{0:T(1024)} copy(f32[1024]{0:T(1024)} %bitcast.19) | data formatting | bytes 8192

commit v3 on v2

--- a/solution.py
+++ b/solution.py
@@ -114,24 +114,27 @@
             remote(chunk_ref(it, inner_at, c), chunk_ref(it, inner_at, c), con_send.at[it, dy, c],
                    con_recv.at[it, dy, c], {"row": place(0, dy)})
 
+    def spread_ref(k, at):
+        return result.at[at, :] if k == 2 else spread.at[k, at, :]
+
     def spread_start(k):
         for dz in range(1, OUTER):
-            remote(spread.at[k, own, :], spread.at[k, own, :], own_send.at[k, dz, 0],
+            remote(spread_ref(k, own), spread_ref(k, own), own_send.at[k, dz, 0],
                    spr_recv.at[k, dz, 0], {"row": place(dz, 0)})
         for dy in range(1, inner):
-            remote(spread.at[k, own, :], spread.at[k, own, :], own_send.at[k, 0, dy],
+            remote(spread_ref(k, own), spread_ref(k, own), own_send.at[k, 0, dy],
                    spr_recv.at[k, 0, dy], {"row": place(0, dy)})
 
     def spread_finish(k):
         for dz in range(1, OUTER):
-            here = spread.at[k, owned(lax.rem(outer_at + OUTER - dz, OUTER), inner_at), :]
+            here = spread_ref(k, owned(lax.rem(outer_at + OUTER - dz, OUTER), inner_at))
             await_recv(here, spr_recv.at[k, dz, 0])
             for dy in range(1, inner):
                 remote(here, here, fwd_send.at[k, dz, dy], spr_recv.at[k, dz, dy], {"row": place(0, dy)})
         for dz in range(OUTER):
             for dy in range(1, inner):
                 there = owned(lax.rem(outer_at + OUTER - dz, OUTER), lax.rem(inner_at + inner - dy, inner))
-                await_recv(spread.at[k, there, :], spr_recv.at[k, dz, dy])
+                await_recv(spread_ref(k, there), spr_recv.at[k, dz, dy])
 
     def build_hot(src):
         line = ids_all[src] - inner_at * part_rows
@@ -177,7 +180,7 @@
         if it == 0:
             mine[...] = new
         else:
-            spread[2, own, :] = new.astype(jnp.bfloat16)
+            result[own, :] = new
             spread_start(2)
         return jnp.sum(((new - old) ** 2).reshape(own_rows // 8, 8, width), axis=0)
 
@@ -266,7 +269,6 @@
     forward(1)
     send_partials(1)
     spread_finish(2)
-    result[...] = spread[2].astype(jnp.float32)
     out_copy = pltpu.make_async_copy(result, primal_out, out_sem)
     out_copy.start()
     total = sum_partials(1)
@@ -312,7 +314,7 @@
             pltpu.VMEM(tall, jnp.float32),
             pltpu.VMEM((inner, blocks // inner, local), jnp.bfloat16),
             pltpu.VMEM((local, blocks), jnp.bfloat16),
-            pltpu.VMEM((3,) + tall, jnp.bfloat16),
+            pltpu.VMEM((2,) + tall, jnp.bfloat16),
             pltpu.VMEM((local, width), jnp.bfloat16),
             pltpu.VMEM((2, inner, local, 2 * width), jnp.bfloat16),
             pltpu.VMEM((inner, 1, local), jnp.int32),

time: 75.3 us -> 76.9 us (1.021)
  Pallas kernels: 69.2 us -> 70.8 us
    pallas_call x1, Pallas kernels: 69.2 us -> 70.8 us  [per_device(): pl.pallas_call(functools.partial(kernel, rows, cols, bands, slots, width,...]
where the time goes in v3:
time: 76.9 us; the launch traced here: 76.7 us
  Pallas kernels  70.8 us (92%)
  local copies, waits for them, and re-layouts  4.57 us (6%)
    pallas_call x1, Pallas kernels, per_device(): pl.pallas_call(functools.partial(kernel, rows, cols, bands, slots, width,...  70.8 us
    unnamed x2, local copies, waits for them, and re-layouts  3.13 us

profile of v3, /device:TPU:0, one launch (start us, length us, event | category | flops | bytes accessed | tf_op | source)
XLA Modules:
  0.0 76.7 jit_solution(5218488172786420243)
XLA Ops:
  0.6 0.7 broadcast_subtract_fusion
  1.3 0.6 reshape.40.ids_row
  2.0 0.8 %reshape.52.ids_col = s32[384,1]{1,0:T(8,128)} reshape(s32[8,48]{1,0:T(8,128)S(1)} %broadcast_subtract_fusion) | data formatting | bytes 3072 | tf_op jit(solution)/shard_map/reshape | solution.py:348
  2.8 70.8 %shard_map.113 = (f32[1024,128]{1,0:T(8,128)}, f32[8,128]{1,0:T(8,128)}) custom-call(bf16[8,48,128,128]{3,2,1,0:T(8,128)(2,1)} %tiles_hbm.1, s32[1,384]{1,0:T(1,128)} %reshape.40.ids_row, s32[384,1]{1,0:T(8,128)} %reshape.52.ids_col, f32[1024,128]{1,0:T(8,128)} %bitcast.10, f32[1024,128]{1,0:T(8,128)} %bitcast.11, f32[1024,128]{1,0:T(8,128)} %bitcast.12, ...), custom_call_target="tpu_custom_call" | custom-call | tf_op jit(solution)/shard_map/pallas_call | solution.py:298
  73.5 1.9 %copy.15 = f32[131072]{0:T(1024)} copy(f32[131072]{0:T(1024)} %bitcast.15) | data formatting | bytes 1048576
  75.4 1.3 %copy.16 = f32[1024]{0:T(1024)} copy(f32[1024]{0:T(1024)} %bitcast.19) | data formatting | bytes 8192
